TPU v7x, 32 devices: a whole 2x2x4 slice. The times are simulated.
32 devices in a mesh: dp: 2 (over y), ctx: 16 (over z, x, core).
Axes of the slice: x: 2, y: 2, z: 4, core: 2. Of those that a mesh axis runs over, the one named last changes fastest.
Arguments:
- query_rows: bfloat16 [32768, 1024], P(('dp', 'ctx')), parts along dimension 0, may hold values from -6 to 6
- key_rows: bfloat16 [32768, 1024], P(('dp', 'ctx')), parts along dimension 0, may hold values from -6 to 6
- value_rows: bfloat16 [32768, 1024], P(('dp', 'ctx')), parts along dimension 0, may hold values from -6 to 6
- lengths: int32 [64], P('dp'), parts along dimension 0, may hold values from 1 to 10240, as said below
- conv_weight: float32 [3, 4, 1024], replicated, may hold values from -3 to 3
- out_gain: float32 [1024], replicated, may hold values from 0.1 to 1.9
Outputs:
- mixed: bfloat16 [32768, 1024], P(('dp', 'ctx')), parts along dimension 0
There are 2 independent parts, one for each index of `dp`. A program takes and returns all parts, laid end to end along the dimension named above; an argument that names none is the same for every part. Nothing has to cross between parts.
Inputs may be any that keep to these rules, and one draw needn't show every extreme that they name: The lengths of one part sum to 16384; the last document has exactly 10240 tokens.
All inputs are finite; a program needn't handle non-finite values.
Results may differ from a plain program's by a relative error of at most 0.0065.
Values may be sent and summed in bfloat16 or wider, within the bound.
A program may use at most 128 MiB of HBM per device.

v0:
```python
import jax
import jax.numpy as jnp
from jax import lax
from jax.sharding import PartitionSpec as P

HEAD = 128


def from_behind(value, axis, steps):
    count = lax.axis_size(axis)
    leading, last = (max(0, -steps), min(count, count - steps))
    return lax.ppermute(value, axis, [(source, source + steps) for source in range(leading, last)])


def doc_lookup(starts, positions):
    return jnp.sum((starts[None, :] <= positions[:, None]).astype(jnp.int32), axis=1) - 1


def features(extended, doc_ext, conv_weight, row_count):
    made = []
    for which in range(3):
        summed = jnp.zeros((row_count, extended[which].shape[1]), jnp.float32)
        for delay in range(4):
            same_doc = (doc_ext[3 - delay : 3 - delay + row_count] == doc_ext[3:]).astype(
                jnp.float32
            )
            shifted = extended[which][3 - delay : 3 - delay + row_count].astype(jnp.float32)
            summed = summed + conv_weight[which, delay][None, :] * shifted * same_doc[:, None]
        made.append(summed)
    return (
        jax.nn.silu(made[0]).astype(jnp.bfloat16),
        jax.nn.silu(made[1]).astype(jnp.bfloat16),
        made[2].astype(jnp.bfloat16),
    )


def mix_block(query_part, key_part, value_part, state_bf, use_in, doc_ids, out_gain):
    row_count = query_part.shape[0]
    block = min(512, row_count)
    pieces = []
    for block_id in range(row_count // block):
        opening = block_id * block
        closing = opening + block
        scores = jnp.einsum(
            "qhd,khd->hqk",
            query_part[opening:closing],
            key_part[:closing],
            preferred_element_type=jnp.float32,
        )
        row_ids = jnp.arange(opening, closing)
        col_ids = jnp.arange(closing)
        allowed = (col_ids[None, :] <= row_ids[:, None]) & (
            doc_ids[:closing][None, :] == doc_ids[opening:closing][:, None]
        )
        weights = jnp.where(allowed[None], scores, 0.0).astype(jnp.bfloat16)
        within = jnp.einsum(
            "hqk,khe->qhe", weights, value_part[:closing], preferred_element_type=jnp.float32
        )
        carried = jnp.einsum(
            "qhd,hde->qhe",
            query_part[opening:closing],
            state_bf,
            preferred_element_type=jnp.float32,
        )
        pieces.append(within + carried * use_in[opening:closing, None, None])
    mixture = jnp.concatenate(pieces, axis=0)
    inverse_rms = lax.rsqrt(jnp.mean(mixture * mixture, axis=-1, keepdims=True) + 1e-06)
    normed = (mixture * inverse_rms).reshape(row_count, -1)
    return (normed * out_gain[None, :]).astype(jnp.bfloat16)


def join_states(earlier, later):
    merged = jnp.where(later[0][0] > 0, later[1], earlier[1] + later[1])
    return (jnp.maximum(earlier[0], later[0]), merged)


def per_device(query_rows, key_rows, value_rows, lengths, conv_weight, out_gain):
    row_count = query_rows.shape[0]
    channels = query_rows.shape[1]
    head_count = channels // HEAD
    offset = lax.axis_index("ctx") * row_count
    starts = jnp.cumsum(lengths) - lengths
    rims = from_behind(
        (query_rows[row_count - 3 :], key_rows[row_count - 3 :], value_rows[row_count - 3 :]),
        "ctx",
        1,
    )
    extended = [
        jnp.concatenate([rims[0], query_rows], axis=0),
        jnp.concatenate([rims[1], key_rows], axis=0),
        jnp.concatenate([rims[2], value_rows], axis=0),
    ]
    positions = offset - 3 + jnp.arange(row_count + 3, dtype=jnp.int32)
    doc_ext = doc_lookup(starts, positions)
    phi_q, phi_k, val = features(extended, doc_ext, conv_weight, row_count)
    doc_ids = doc_ext[3:]
    phi_q = phi_q.reshape(row_count, head_count, HEAD)
    phi_k = phi_k.reshape(row_count, head_count, HEAD)
    val = val.reshape(row_count, head_count, HEAD)
    tail_mask = (doc_ids == doc_ids[-1]).astype(jnp.bfloat16)
    tail_state = jnp.einsum(
        "thd,the->hde", phi_k * tail_mask[:, None, None], val, preferred_element_type=jnp.float32
    )
    restart = (
        jnp.any((starts >= offset) & (starts < offset + row_count)).astype(jnp.float32).reshape(1)
    )
    moved = from_behind((restart, tail_state), "ctx", 1)
    axis_count = lax.axis_size("ctx")
    reach = (axis_count * 5 + 7) // 8
    rounds = max(reach - 1, 0).bit_length()
    for level in range(rounds):
        received = from_behind((moved[0], moved[1]), "ctx", 1 << level)
        moved = join_states(received, moved)
    incoming = moved[1]
    opens_here = jnp.any(starts == offset)
    use_in = ((doc_ids == doc_ids[0]) & jnp.logical_not(opens_here)).astype(jnp.float32)
    return mix_block(phi_q, phi_k, val, incoming.astype(jnp.bfloat16), use_in, doc_ids, out_gain)


def solution(mesh):
    return jax.shard_map(
        per_device,
        mesh=mesh,
        in_specs=(
            P(("dp", "ctx"), None),
            P(("dp", "ctx"), None),
            P(("dp", "ctx"), None),
            P("dp"),
            P(),
            P(),
        ),
        out_specs=P(("dp", "ctx"), None),
        check_vma=False,
    )
```

profile of v0, /device:TPU:24, one launch (start us, length us, event | category | flops | bytes accessed | tf_op | source)
XLA Modules:
  0.0 150.6 jit_solution(5007534312085816447)
XLA Ops:
  0.0 0.7 slice.156
  0.7 0.2 copy.77
  0.9 1.9 %collective-permute-start = (bf16[3,1024]{0,1:T(8,128)(2,1)S(1)}, bf16[3,1024]{0,1:T(8,128)(2,1)S(1)}, u32[]{:S(2)}, u32[]{:S(2)}) collective-permute-start(bf16[3,1024]{0,1:T(8,128)(2,1)S(1)} %copy.77), channel_id=1, source_target_pairs={{0,1},{1,2},{2,3},{3,4},{4,5},{5,6},{6,7},{7,8},{8,9},{9,10},{10,1... | collective-permute-start | bytes 18440 | tf_op jit(solution)/shard_map/ppermute | solution.py:12
  2.9 0.7 slice.181
  3.6 0.2 copy.84
  3.8 3.5 %collective-permute-start.2 = (bf16[3,1024]{0,1:T(8,128)(2,1)S(1)}, bf16[3,1024]{0,1:T(8,128)(2,1)S(1)}, u32[]{:S(2)}, u32[]{:S(2)}) collective-permute-start(bf16[3,1024]{0,1:T(8,128)(2,1)S(1)} %copy.84), channel_id=1, source_target_pairs={{0,1},{1,2},{2,3},{3,4},{4,5},{5,6},{6,7},{7,8},{8,9},{9,10},{10,1... | collective-permute-start | bytes 18440 | tf_op jit(solution)/shard_map/ppermute | solution.py:12
  7.3 0.7 copy.79
  8.1 0.1 reduce-window.9
  8.1 0.1 reduce
  8.2 1.4 compare_reduce_fusion
  9.6 0.1 convert_reduce_fusion
  9.7 0.7 fusion.29
  11.0 1.0 fusion.27
  12.0 1.3 and_convert_fusion
  13.3 3.9 %copy.76 = bf16[1024,1024]{0,1:T(8,128)(2,1)} copy(bf16[1024,1024]{1,0:T(8,128)(2,1)} %param.8) | data formatting | bytes 4194304 | tf_op args[2]
  17.3 2.9 %copy.83 = bf16[1024,1024]{0,1:T(8,128)(2,1)S(1)} copy(bf16[1024,1024]{1,0:T(8,128)(2,1)} %param.7) | data formatting | bytes 4194304 | tf_op args[1]
  20.1 0.0 collective-permute-done
  20.2 8.9 %add_convert_fusion = bf16[1024,1024]{0,1:T(8,128)(2,1)S(1)} fusion(bf16[1024,1024]{0,1:T(8,128)(2,1)} %copy.76, bf16[3,1024]{0,1:T(8,128)(2,1)S(1)} %collective-permute-done, f32[1024]{0:T(1024)S(1)} %get-tuple-element.26, f32[1024]{0:T(1024)S(1)} %bitcast.73, f32[1024]{0:T(1024)S(1)} %get-tuple-element.27, f32[1024]{0:T(1024)S(1)} %bitcast.74, ...), kind=kLoop, calls=%fused_computation.11 | loop fusion | flops 25165824 | bytes 4229120 | tf_op jit(solution)/shard_map/convert_element_type | solution.py:33
  29.0 4.5 %multiply_convert_fusion = bf16[1024,1024]{0,1:T(8,128)(2,1)S(1)} fusion(bf16[1024,1024]{0,1:T(8,128)(2,1)S(1)} %copy.83, bf16[3,1024]{0,1:T(8,128)(2,1)S(1)} %collective-permute-done.2, f32[1024]{0:T(1024)S(1)} %bitcast.71, f32[1024]{0:T(1024)S(1)} %bitcast.72, f32[1024]{0:T(1024)S(1)} %bitcast.69, f32[1024]{0:T(1024)S(1)} %bitcast.70, ...), kind=kLoop, calls=%fused_computation.9 | loop fusion | flops 29360128 | bytes 4229120 | tf_op jit(solution)/shard_map/convert_element_type | solution.py:32
  33.6 0.7 fusion.15
  34.3 1.9 %collective-permute-start.7 = (f32[8,128,128]{2,1,0:T(8,128)S(1)}, f32[8,128,128]{2,1,0:T(8,128)S(1)}, u32[]{:S(2)}, u32[]{:S(2)}) collective-permute-start(f32[8,128,128]{2,1,0:T(8,128)S(1)} %fusion.15), channel_id=1, source_target_pairs={{0,1},{1,2},{2,3},{3,4},{4,5},{5,6},{6,7},{7,8},{8,9},{9,10},{10,1... | collective-permute-start | bytes 1572872 | tf_op jit(solution)/shard_map/ppermute | solution.py:12
  36.2 9.5 %collective-permute-done.7 = f32[8,128,128]{2,1,0:T(8,128)S(1)} collective-permute-done((f32[8,128,128]{2,1,0:T(8,128)S(1)}, f32[8,128,128]{2,1,0:T(8,128)S(1)}, u32[]{:S(2)}, u32[]{:S(2)}) %collective-permute-start.7) | collective-permute-done | bytes 524320 | tf_op jit(solution)/shard_map/ppermute | solution.py:12
  45.7 1.9 %collective-permute-start.8 = (f32[8,128,128]{2,1,0:T(8,128)S(1)}, f32[8,128,128]{2,1,0:T(8,128)S(1)}, u32[]{:S(2)}, u32[]{:S(2)}) collective-permute-start(f32[8,128,128]{2,1,0:T(8,128)S(1)} %collective-permute-done.7), channel_id=1, source_target_pairs={{0,1},{1,2},{2,3},{3,4},{4,5},{5,6},{6,7},{7,8},{8,9},{9,10},{10,1... | collective-permute-start | bytes 1572872 | tf_op jit(solution)/shard_map/ppermute | solution.py:12
  48.3 2.9 %collective-permute-start.3 = (f32[1]{0:T(128)}, f32[1]{0:T(128)}, u32[]{:S(2)}, u32[]{:S(2)}) collective-permute-start(f32[1]{0:T(128)} %bitcast.16), channel_id=1, source_target_pairs={{0,1},{1,2},{2,3},{3,4},{4,5},{5,6},{6,7},{7,8},{8,9},{9,10},{10,1... | collective-permute-start | bytes 20 | tf_op jit(solution)/shard_map/ppermute | solution.py:12
  51.1 6.1 %collective-permute-done.3 = f32[1]{0:T(128)} collective-permute-done((f32[1]{0:T(128)}, f32[1]{0:T(128)}, u32[]{:S(2)}, u32[]{:S(2)}) %collective-permute-start.3) | collective-permute-done | bytes 36 | tf_op jit(solution)/shard_map/ppermute | solution.py:12
  57.8 0.1 add_select_fusion.3
  57.9 1.9 %collective-permute-start.9 = (f32[8,128,128]{2,1,0:T(8,128)S(1)}, f32[8,128,128]{2,1,0:T(8,128)S(1)}, u32[]{:S(2)}, u32[]{:S(2)}) collective-permute-start(f32[8,128,128]{2,1,0:T(8,128)S(1)} %add_select_fusion.3), channel_id=1, source_target_pairs={{0,2},{1,3},{2,4},{3,5},{4,6},{5,7},{6,8},{7,9},{8,10},{9,11},{10,... | collective-permute-start | bytes 1572872 | tf_op jit(solution)/shard_map/ppermute | solution.py:12
  59.8 0.7 slice.171
  60.6 0.9 copy.81
  61.5 1.9 %collective-permute-start.1 = (bf16[3,1024]{0,1:T(8,128)(2,1)}, bf16[3,1024]{0,1:T(8,128)(2,1)S(1)}, u32[]{:S(2)}, u32[]{:S(2)}) collective-permute-start(bf16[3,1024]{0,1:T(8,128)(2,1)} %copy.81), channel_id=1, source_target_pairs={{0,1},{1,2},{2,3},{3,4},{4,5},{5,6},{6,7},{7,8},{8,9},{9,10},{10,1... | collective-permute-start | bytes 18440 | tf_op jit(solution)/shard_map/ppermute | solution.py:12
  63.4 0.1 fusion.28
  63.4 1.9 %collective-permute-start.4 = (f32[1]{0:T(128)}, f32[1]{0:T(128)}, u32[]{:S(2)}, u32[]{:S(2)}) collective-permute-start(f32[1]{0:T(128)} %collective-permute-done.3), channel_id=1, source_target_pairs={{0,1},{1,2},{2,3},{3,4},{4,5},{5,6},{6,7},{7,8},{8,9},{9,10},{10,1... | collective-permute-start | bytes 20 | tf_op jit(solution)/shard_map/ppermute | solution.py:12
  65.4 7.8 %collective-permute-done.4 = f32[1]{0:T(128)} collective-permute-done((f32[1]{0:T(128)}, f32[1]{0:T(128)}, u32[]{:S(2)}, u32[]{:S(2)}) %collective-permute-start.4) | collective-permute-done | bytes 36 | tf_op jit(solution)/shard_map/ppermute | solution.py:12
  74.4 0.1 add_select_fusion.2
  74.5 1.3 collective-permute-start.10
  75.8 2.9 %copy.80 = bf16[1024,1024]{0,1:T(8,128)(2,1)S(1)} copy(bf16[1024,1024]{1,0:T(8,128)(2,1)} %param.6) | data formatting | bytes 4194304 | tf_op args[0]
  78.7 0.1 slice.199
  78.7 0.9 fusion.19
  79.7 1.3 fusion.17
  81.0 3.3 %collective-permute-start.5 = (f32[1]{0:T(128)}, f32[1]{0:T(128)}, u32[]{:S(2)}, u32[]{:S(2)}) collective-permute-start(f32[1]{0:T(128)} %max.9), channel_id=1, source_target_pairs={{0,2},{1,3},{2,4},{3,5},{4,6},{5,7},{6,8},{7,9},{8,10},{9,11},{10,... | collective-permute-start | bytes 20 | tf_op jit(solution)/shard_map/ppermute | solution.py:12
  84.3 4.0 %collective-permute-done.5 = f32[1]{0:T(128)} collective-permute-done((f32[1]{0:T(128)}, f32[1]{0:T(128)}, u32[]{:S(2)}, u32[]{:S(2)}) %collective-permute-start.5) | collective-permute-done | bytes 36 | tf_op jit(solution)/shard_map/ppermute | solution.py:12
  88.9 1.3 collective-permute-start.6
  90.2 4.1 %collective-permute-done.6 = f32[1]{0:T(128)} collective-permute-done((f32[1]{0:T(128)}, f32[1]{0:T(128)}, u32[]{:S(2)}, u32[]{:S(2)}) %collective-permute-start.6) | collective-permute-done | bytes 36 | tf_op jit(solution)/shard_map/ppermute | solution.py:12
  95.0 0.0 collective-permute-done.10
  95.0 0.1 add_select_fusion.1
  95.0 1.5 collective-permute-start.11
  96.5 4.5 %multiply_convert_fusion.1 = bf16[1024,1024]{0,1:T(8,128)(2,1)S(1)} fusion(bf16[1024,1024]{0,1:T(8,128)(2,1)S(1)} %copy.80, bf16[3,1024]{0,1:T(8,128)(2,1)S(1)} %collective-permute-done.1, f32[1024]{0:T(1024)S(1)} %bitcast.66, f32[1024]{0:T(1024)S(1)} %bitcast.67, f32[1024]{0:T(1024)S(1)} %bitcast.68, f32[1024]{0:T(1024)S(1)} %bitcast.65, ...), kind=kLoop, calls=%fused_computation.10 | loop fusion | flops 29360128 | bytes 4229120 | tf_op jit(solution)/shard_map/convert_element_type | solution.py:31
  101.1 1.1 slice.204
  102.2 1.1 slice.215
  103.3 0.2 fusion.26
  103.5 16.5 %collective-permute-done.11 = f32[8,128,128]{2,1,0:T(8,128)S(1)} collective-permute-done((f32[8,128,128]{2,1,0:T(8,128)S(1)}, f32[8,128,128]{2,1,0:T(8,128)S(1)}, u32[]{:S(2)}, u32[]{:S(2)}) %collective-permute-start.11) | collective-permute-done | bytes 524320 | tf_op jit(solution)/shard_map/ppermute | solution.py:12
  119.9 0.1 fusion.20
  120.0 1.8 %fusion.32 = f32[8,128,512]{2,1,0:T(8,128)} fusion(bf16[8,128,128]{2,1,0:T(8,128)(2,1)S(1)} %fusion.20, bf16[512,8,128]{0,2,1:T(8,128)(2,1)S(1)} %bitcast.61), kind=kOutput, calls=%fused_computation.73 | convolution fusion | flops 134217728 | bytes 3407872 | tf_op jit(solution)/shard_map/qhd,hde->qhe/dot_general | solution.py:59
  121.8 1.8 %fusion.31 = f32[8,128,512]{2,1,0:T(8,128)} fusion(bf16[8,128,128]{2,1,0:T(8,128)(2,1)S(1)} %fusion.20, bf16[512,8,128]{0,2,1:T(8,128)(2,1)S(1)} %bitcast.59), kind=kOutput, calls=%fused_computation.72 | convolution fusion | flops 134217728 | bytes 3407872 | tf_op jit(solution)/shard_map/qhd,hde->qhe/dot_general | solution.py:59
  123.6 8.5 %multiply_add_fusion = f32[8,128,512]{2,1,0:T(8,128)S(1)} fusion(f32[8,128,512]{2,1,0:T(8,128)} %fusion.32, bf16[1024,8,128]{0,2,1:T(8,128)(2,1)} %bitcast.56, bf16[512,8,128]{0,2,1:T(8,128)(2,1)} %bitcast.62, bf16[1024,8,128]{0,2,1:T(8,128)(2,1)} %bitcast.58, pred[512,1024]{1,0:T(8,128)(4,1)} %fusion.17, f32[512]{0:T(512)S(1)} %get-tuple-element.32), kind=kOutput, calls=%fused_computation.36 | convolution fusion | flops 2156920832 | bytes 9963520 | tf_op jit(solution)/shard_map/hqk,khe->qhe/dot_general | solution.py:56
  132.1 6.9 %multiply_add_fusion.1 = f32[8,128,512]{2,1,0:T(8,128)} fusion(f32[8,128,512]{2,1,0:T(8,128)} %fusion.31, f32[512]{0:T(512)S(1)} %get-tuple-element.31, bf16[512,8,128]{0,2,1:T(8,128)(2,1)} %bitcast.63, pred[512,512]{1,0:T(8,128)(4,1)S(1)} %copy-done.7, bf16[512,8,128]{0,2,1:T(8,128)(2,1)S(1)} %bitcast.60, bf16[512,8,128]{0,2,1:T(8,128)(2,1)} %bitcast.64), kind=kOutput, calls=%fused_computation.38 | convolution fusion | flops 1078984704 | bytes 7604224 | tf_op jit(solution)/shard_map/hqk,khe->qhe/dot_general | solution.py:56
  139.1 2.1 %fusion.3 = f32[1024,8]{0,1:T(8,128)S(1)} fusion(f32[512,8,128]{0,2,1:T(8,128)S(1)} %bitcast.51, f32[512,8,128]{0,2,1:T(8,128)} %bitcast.53), kind=kLoop, calls=%fused_computation.7 | loop fusion | flops 3137536 | bytes 4227072 | tf_op jit(solution)/shard_map/reduce_sum | solution.py:67
  141.2 0.2 copy.97
  141.4 1.9 %copy.96 = f32[512,1024]{1,0:T(8,128)S(1)} copy(f32[512,1024]{0,1:T(8,128)} %bitcast.52) | data formatting | bytes 4194304 | tf_op jit(solution)/shard_map/concatenate | solution.py:66
  143.4 0.0 copy-start.8
  143.4 2.9 %copy.95 = f32[512,1024]{1,0:T(8,128)} copy(f32[512,1024]{0,1:T(8,128)} %bitcast.54) | data formatting | bytes 4194304 | tf_op jit(solution)/shard_map/concatenate | solution.py:66
  146.3 1.1 mul.311
  147.5 0.4 copy-done
  147.9 2.7 %fusion.2 = bf16[1024,1024]{1,0:T(8,128)(2,1)} fusion(f32[128,8,8,128]{3,2,1,0:T(8,128)S(1)} %bitcast.50, f32[512,1024]{1,0:T(8,128)S(1)} %copy.96, f32[512,1024]{1,0:T(8,128)S(1)} %copy-done, f32[1024]{0:T(1024)S(1)} %copy-done.8), kind=kLoop, calls=%fused_computation.5 | loop fusion | flops 4194304 | bytes 10489856 | tf_op jit(solution)/shard_map/convert_element_type | solution.py:69
  (25 shorter events, 0.1 us)
Async XLA Ops:
  0.9 19.2 %collective-permute-start = (bf16[3,1024]{0,1:T(8,128)(2,1)S(1)}, bf16[3,1024]{0,1:T(8,128)(2,1)S(1)}, u32[]{:S(2)}, u32[]{:S(2)}) collective-permute-start(bf16[3,1024]{0,1:T(8,128)(2,1)S(1)} %copy.77), channel_id=1, source_target_pairs={{0,1},{1,2},{2,3},{3,4},{4,5},{5,6},{6,7},{7,8},{8,9},{9,10},{10,1... | collective-permute-start | bytes 18440 | tf_op jit(solution)/shard_map/ppermute | solution.py:12
  3.8 25.2 %collective-permute-start.2 = (bf16[3,1024]{0,1:T(8,128)(2,1)S(1)}, bf16[3,1024]{0,1:T(8,128)(2,1)S(1)}, u32[]{:S(2)}, u32[]{:S(2)}) collective-permute-start(bf16[3,1024]{0,1:T(8,128)(2,1)S(1)} %copy.84), channel_id=1, source_target_pairs={{0,1},{1,2},{2,3},{3,4},{4,5},{5,6},{6,7},{7,8},{8,9},{9,10},{10,1... | collective-permute-start | bytes 18440 | tf_op jit(solution)/shard_map/ppermute | solution.py:12
  29.0 5.3 %copy-start.2 = (bf16[1024,1024]{0,1:T(8,128)(2,1)}, bf16[1024,1024]{0,1:T(8,128)(2,1)S(1)}, u32[]{:S(2)}) copy-start(bf16[1024,1024]{0,1:T(8,128)(2,1)S(1)} %add_convert_fusion) | copy-start | bytes 6291460
  33.6 2.7 %copy-start.4 = (bf16[1024,1024]{0,1:T(8,128)(2,1)}, bf16[1024,1024]{0,1:T(8,128)(2,1)S(1)}, u32[]{:S(2)}) copy-start(bf16[1024,1024]{0,1:T(8,128)(2,1)S(1)} %multiply_convert_fusion) | copy-start | bytes 6291460
  34.3 11.4 %collective-permute-start.7 = (f32[8,128,128]{2,1,0:T(8,128)S(1)}, f32[8,128,128]{2,1,0:T(8,128)S(1)}, u32[]{:S(2)}, u32[]{:S(2)}) collective-permute-start(f32[8,128,128]{2,1,0:T(8,128)S(1)} %fusion.15), channel_id=1, source_target_pairs={{0,1},{1,2},{2,3},{3,4},{4,5},{5,6},{6,7},{7,8},{8,9},{9,10},{10,1... | collective-permute-start | bytes 1572872 | tf_op jit(solution)/shard_map/ppermute | solution.py:12
  45.7 12.1 %collective-permute-start.8 = (f32[8,128,128]{2,1,0:T(8,128)S(1)}, f32[8,128,128]{2,1,0:T(8,128)S(1)}, u32[]{:S(2)}, u32[]{:S(2)}) collective-permute-start(f32[8,128,128]{2,1,0:T(8,128)S(1)} %collective-permute-done.7), channel_id=1, source_target_pairs={{0,1},{1,2},{2,3},{3,4},{4,5},{5,6},{6,7},{7,8},{8,9},{9,10},{10,1... | collective-permute-start | bytes 1572872 | tf_op jit(solution)/shard_map/ppermute | solution.py:12
  48.3 9.0 %collective-permute-start.3 = (f32[1]{0:T(128)}, f32[1]{0:T(128)}, u32[]{:S(2)}, u32[]{:S(2)}) collective-permute-start(f32[1]{0:T(128)} %bitcast.16), channel_id=1, source_target_pairs={{0,1},{1,2},{2,3},{3,4},{4,5},{5,6},{6,7},{7,8},{8,9},{9,10},{10,1... | collective-permute-start | bytes 20 | tf_op jit(solution)/shard_map/ppermute | solution.py:12
  57.9 16.5 %collective-permute-start.9 = (f32[8,128,128]{2,1,0:T(8,128)S(1)}, f32[8,128,128]{2,1,0:T(8,128)S(1)}, u32[]{:S(2)}, u32[]{:S(2)}) collective-permute-start(f32[8,128,128]{2,1,0:T(8,128)S(1)} %add_select_fusion.3), channel_id=1, source_target_pairs={{0,2},{1,3},{2,4},{3,5},{4,6},{5,7},{6,8},{7,9},{8,10},{9,11},{10,... | collective-permute-start | bytes 1572872 | tf_op jit(solution)/shard_map/ppermute | solution.py:12
  61.5 35.1 %collective-permute-start.1 = (bf16[3,1024]{0,1:T(8,128)(2,1)}, bf16[3,1024]{0,1:T(8,128)(2,1)S(1)}, u32[]{:S(2)}, u32[]{:S(2)}) collective-permute-start(bf16[3,1024]{0,1:T(8,128)(2,1)} %copy.81), channel_id=1, source_target_pairs={{0,1},{1,2},{2,3},{3,4},{4,5},{5,6},{6,7},{7,8},{8,9},{9,10},{10,1... | collective-permute-start | bytes 18440 | tf_op jit(solution)/shard_map/ppermute | solution.py:12
  63.4 9.7 %collective-permute-start.4 = (f32[1]{0:T(128)}, f32[1]{0:T(128)}, u32[]{:S(2)}, u32[]{:S(2)}) collective-permute-start(f32[1]{0:T(128)} %collective-permute-done.3), channel_id=1, source_target_pairs={{0,1},{1,2},{2,3},{3,4},{4,5},{5,6},{6,7},{7,8},{8,9},{9,10},{10,1... | collective-permute-start | bytes 20 | tf_op jit(solution)/shard_map/ppermute | solution.py:12
  74.5 20.5 %collective-permute-start.10 = (f32[8,128,128]{2,1,0:T(8,128)S(1)}, f32[8,128,128]{2,1,0:T(8,128)S(1)}, u32[]{:S(2)}, u32[]{:S(2)}) collective-permute-start(f32[8,128,128]{2,1,0:T(8,128)S(1)} %add_select_fusion.2), channel_id=1, source_target_pairs={{0,4},{1,5},{2,6},{3,7},{4,8},{5,9},{6,10},{7,11},{8,12},{9,13},{1... | collective-permute-start | bytes 1572872 | tf_op jit(solution)/shard_map/ppermute | solution.py:12
  78.7 22.4 %copy-start.3 = (bf16[1024,1024]{0,1:T(8,128)(2,1)S(1)}, bf16[1024,1024]{0,1:T(8,128)(2,1)}, u32[]{:S(2)}) copy-start(bf16[1024,1024]{0,1:T(8,128)(2,1)} %copy-done.2) | copy-start | bytes 6291460
  81.0 21.2 %copy-start.5 = (bf16[1024,1024]{0,1:T(8,128)(2,1)S(1)}, bf16[1024,1024]{0,1:T(8,128)(2,1)}, u32[]{:S(2)}) copy-start(bf16[1024,1024]{0,1:T(8,128)(2,1)} %copy-done.4) | copy-start | bytes 6291460
  81.0 7.3 %collective-permute-start.5 = (f32[1]{0:T(128)}, f32[1]{0:T(128)}, u32[]{:S(2)}, u32[]{:S(2)}) collective-permute-start(f32[1]{0:T(128)} %max.9), channel_id=1, source_target_pairs={{0,2},{1,3},{2,4},{3,5},{4,6},{5,7},{6,8},{7,9},{8,10},{9,11},{10,... | collective-permute-start | bytes 20 | tf_op jit(solution)/shard_map/ppermute | solution.py:12
  88.9 5.4 %collective-permute-start.6 = (f32[1]{0:T(128)}, f32[1]{0:T(128)}, u32[]{:S(2)}, u32[]{:S(2)}) collective-permute-start(f32[1]{0:T(128)} %max.10), channel_id=1, source_target_pairs={{0,4},{1,5},{2,6},{3,7},{4,8},{5,9},{6,10},{7,11},{8,12},{9,13},{1... | collective-permute-start | bytes 20 | tf_op jit(solution)/shard_map/ppermute | solution.py:12
  95.0 24.9 %collective-permute-start.11 = (f32[8,128,128]{2,1,0:T(8,128)S(1)}, f32[8,128,128]{2,1,0:T(8,128)S(1)}, u32[]{:S(2)}, u32[]{:S(2)}) collective-permute-start(f32[8,128,128]{2,1,0:T(8,128)S(1)} %add_select_fusion.1), channel_id=1, source_target_pairs={{0,8},{1,9},{2,10},{3,11},{4,12},{5,13},{6,14},{7,15},{16,24},{17,... | collective-permute-start | bytes 1572872 | tf_op jit(solution)/shard_map/ppermute | solution.py:12
  103.5 20.2 %copy-start.6 = (bf16[512,1024]{0,1:T(8,128)(2,1)}, bf16[512,1024]{0,1:T(8,128)(2,1)S(1)}, u32[]{:S(2)}) copy-start(bf16[512,1024]{0,1:T(8,128)(2,1)S(1)} %get-tuple-element.9) | copy-start | bytes 3145732
  123.6 8.5 %copy-start.7 = (pred[512,512]{1,0:T(8,128)(4,1)S(1)}, pred[512,512]{1,0:T(8,128)(4,1)}, u32[]{:S(2)}) copy-start(pred[512,512]{1,0:T(8,128)(4,1)} %fusion.19) | copy-start | bytes 786436
  132.1 7.0 %copy-start.1 = (f32[8,128,512]{2,1,0:T(8,128)}, f32[8,128,512]{2,1,0:T(8,128)S(1)}, u32[]{:S(2)}) copy-start(f32[8,128,512]{2,1,0:T(8,128)S(1)} %multiply_add_fusion) | copy-start | bytes 6291460
  143.4 4.1 %copy-start.8 = (f32[1024]{0:T(1024)S(1)}, f32[1024]{0:T(1024)}, u32[]{:S(2)}) copy-start(f32[1024]{0:T(1024)} %param.11) | copy-start | bytes 12292
  146.3 1.6 %copy-start = (f32[512,1024]{1,0:T(8,128)S(1)}, f32[512,1024]{1,0:T(8,128)}, u32[]{:S(2)}) copy-start(f32[512,1024]{1,0:T(8,128)} %copy.95) | copy-start | bytes 6291460
where the time goes:
time: 152 us; the launch traced here: 151 us
  waiting for transfers between devices  47.9 us (32%)
  other arithmetic  28.1 us (18%)
  starting transfers between devices  25.2 us (17%)
  local copies, waits for them, and re-layouts  24.7 us (16%)
  matrix products  19.7 us (13%)
  between operations  4.85 us (3%)
    ppermute x12, waiting for transfers between devices, from_behind(): lax.ppermute(value, axis, [(source, source + steps) for source in range(l...  47.9 us
    ppermute x12, starting transfers between devices, from_behind(): lax.ppermute(value, axis, [(source, source + steps) for source in range(l...  25.2 us
    dot_general x2, matrix products, mix_block(): jnp.einsum('hqk,khe->qhe', weights, value_part[:closing], preferred_eleme...  15.4 us
    unnamed x21, local copies, waits for them, and re-layouts  10.1 us
    convert_element_type x1, other arithmetic, features(): made[2].astype(jnp.bfloat16)  8.87 us
    concatenate x2, local copies, waits for them, and re-layouts, mix_block(): mixture = jnp.concatenate(pieces, axis=0)  4.86 us
    convert_element_type x1, other arithmetic, features(): jax.nn.silu(made[0]).astype(jnp.bfloat16)  4.51 us
    convert_element_type x1, other arithmetic, features(): jax.nn.silu(made[1]).astype(jnp.bfloat16)  4.51 us
  transfers between devices with their start and end apart: 12, of which 6 were waited for; matrix products, arithmetic and copies ran while one was open for 24% of the time, Pallas kernels for 0%

commit v1 on v0

v1 whole, which is shorter than its diff:
```python
import functools

import jax
import jax.numpy as jnp
from jax import lax
from jax.experimental import pallas as pl
from jax.experimental.pallas import tpu as pltpu
from jax.sharding import PartitionSpec as P

HEAD = 128
PAD = 16
MESH = pl.DeviceIdType.MESH
F32 = jnp.float32
BF16 = jnp.bfloat16


def lanes(head):
    return pl.ds(pl.multiple_of(head * HEAD, HEAD), HEAD)


def iota(shape, dim):
    return lax.broadcasted_iota(jnp.int32, shape, dim).astype(F32)


def kernel(
    n, q_hbm, k_hbm, v_hbm, len_ref, cw_ref, gain_ref, out_ref,
    rows_in, phi, mix, masks, allow, tail, gathered, scanned, carried,
    load_sem, halo_send, halo_recv, send_sem, recv_sem,
):
    me = lax.axis_index("ctx")
    T, width = q_hbm.shape
    heads = width // HEAD
    R = width // n
    ndoc = len_ref.shape[1]
    inputs = (q_hbm, k_hbm, v_hbm)

    def load(w):
        return pltpu.make_async_copy(inputs[w], rows_in.at[w, pl.ds(PAD, T)], load_sem.at[w])

    for w in (1, 2, 0):
        load(w).start()

    barrier = pltpu.get_barrier_semaphore()

    @pl.loop(1, n)
    def _(k):
        pl.semaphore_signal(
            barrier, inc=1, device_id={"ctx": lax.rem(me + k, n)}, device_id_type=MESH
        )

    sub = lax.broadcasted_iota(jnp.int32, (ndoc, ndoc), 0)
    lan = lax.broadcasted_iota(jnp.int32, (ndoc, ndoc), 1)
    lens = len_ref[...].astype(F32)
    col = jnp.sum(jnp.where(lan < sub, lens, 0.0), axis=1, keepdims=True)
    starts = jnp.sum(jnp.where(lan == sub, col, 0.0), axis=0, keepdims=True)
    offset = (me * T).astype(F32)
    end = offset + (T - 1)
    last_start = jnp.max(jnp.where(starts <= end, starts, -1.0), axis=1, keepdims=True)

    MC = 128

    @pl.loop(0, T // MC)
    def _(c):
        r0 = pl.multiple_of(c * MC, MC)
        local = (r0 + lax.broadcasted_iota(jnp.int32, (MC, 1), 0)).astype(F32)
        pos = local + offset
        mine = jnp.max(jnp.where(starts <= pos, starts, -1.0), axis=1, keepdims=True)
        depth = jnp.broadcast_to(pos - mine, (MC, HEAD))
        rows = pl.ds(r0, MC)
        for j in range(1, 4):
            masks[j - 1, rows, :] = (depth >= j).astype(F32)
        masks[3, rows, :] = (depth > local).astype(F32)
        for piece in range(T // HEAD):
            gap = local - (iota((MC, HEAD), 1) + piece * HEAD)
            ok = (gap >= 0.0) & (gap <= depth)
            allow[rows, piece * HEAD : (piece + 1) * HEAD] = jnp.where(ok, 1.0, 0.0).astype(BF16)

    C = 64

    def conv(w, c):
        r0 = pl.multiple_of(c * C, C)
        rows = pl.ds(r0, C)
        m = [masks[j, rows, :] for j in range(3)]
        for h in range(heads):
            cols = slice(h * HEAD, (h + 1) * HEAD)
            ext = rows_in[w, pl.ds(r0, C + PAD), cols].astype(F32)
            scale = 1.0 if w == 2 else 0.5
            acc = ext[PAD:] * (cw_ref[w, 0:1, cols] * scale)
            for j in range(1, 4):
                acc += (ext[PAD - j : PAD - j + C] * m[j - 1]) * (cw_ref[w, j : j + 1, cols] * scale)
            if w < 2:
                acc = acc + acc * jnp.tanh(acc)
            phi[w, rows, cols] = acc.astype(BF16)

    chunks = T // C
    half = chunks // 2

    load(1).wait()
    load(2).wait()

    @pl.loop(0, half)
    def _(i):
        conv(1, chunks - 1 - i)
        conv(2, chunks - 1 - i)

    pl.semaphore_wait(barrier, n - 1)
    nxt = lax.rem(me + 1, n)

    def halo(w):
        return pltpu.make_async_remote_copy(
            src_ref=inputs[w].at[pl.ds(T - PAD, PAD)],
            dst_ref=rows_in.at[w, pl.ds(0, PAD)],
            send_sem=halo_send.at[w],
            recv_sem=halo_recv.at[w],
            device_id={"ctx": nxt},
            device_id_type=MESH,
        )

    for w in (1, 2, 0):
        halo(w).start()

    @pl.loop(half, chunks - 1)
    def _(i):
        conv(1, chunks - 1 - i)
        conv(2, chunks - 1 - i)

    halo(1).wait_recv()
    halo(2).wait_recv()
    conv(1, 0)
    conv(2, 0)

    tail_rows = (iota((T, HEAD), 0) + offset) >= last_start

    @pl.loop(0, heads)
    def _(h):
        key = jnp.where(tail_rows, phi[1, :, lanes(h)].astype(F32), 0.0).astype(BF16)
        state = lax.dot_general(
            key, phi[2, :, lanes(h)], (((0,), (0,)), ((), ())), preferred_element_type=F32
        )
        tail[lanes(h), :] = state.astype(BF16)

    def slice_rows(d):
        return pl.ds(pl.multiple_of(d * R, R), R)

    def give(k):
        to = lax.rem(me + k, n)
        return pltpu.make_async_remote_copy(
            src_ref=tail.at[slice_rows(to)],
            dst_ref=gathered.at[slice_rows(me)],
            send_sem=send_sem.at[0, k],
            recv_sem=recv_sem.at[0, k],
            device_id={"ctx": to},
            device_id_type=MESH,
        )

    def back(k):
        to = lax.rem(me + k, n)
        return pltpu.make_async_remote_copy(
            src_ref=scanned.at[slice_rows(to)],
            dst_ref=carried.at[slice_rows(me)],
            send_sem=send_sem.at[1, k],
            recv_sem=recv_sem.at[1, k],
            device_id={"ctx": to},
            device_id_type=MESH,
        )

    @pl.loop(1, n)
    def _(k):
        give(k).start()

    gathered[slice_rows(me), :] = tail[slice_rows(me), :]

    load(0).wait()

    @pl.loop(0, chunks - 1)
    def _(i):
        conv(0, chunks - 1 - i)

    halo(0).wait_recv()
    conv(0, 0)

    B = 256

    def attend(i):
        lo, hi = i * B, (i + 1) * B

        @pl.loop(0, heads)
        def _(h):
            score = lax.dot_general(
                phi[0, lo:hi, lanes(h)], phi[1, 0:hi, lanes(h)],
                (((1,), (1,)), ((), ())), preferred_element_type=F32,
            )
            weights = score.astype(BF16) * allow[lo:hi, 0:hi]
            mix[lo:hi, lanes(h)] = jnp.dot(
                weights, phi[2, 0:hi, lanes(h)], preferred_element_type=F32
            )

    tiles = T // B
    attend(tiles - 1)

    @pl.loop(1, n)
    def _(k):
        give(k).wait_recv()

    def step(b, state):
        scanned[slice_rows(b), :] = state.astype(BF16)
        first = (b * T).astype(F32)
        inside = (starts >= first) & (starts < first + T)
        hit = jnp.max(jnp.where(inside, 1.0, 0.0), axis=1, keepdims=True)
        return state * (1.0 - hit) + gathered[slice_rows(b), :].astype(F32)

    lax.fori_loop(0, n, step, jnp.zeros((R, HEAD), F32))

    @pl.loop(1, n)
    def _(k):
        back(k).start()

    carried[slice_rows(me), :] = scanned[slice_rows(me), :]

    for i in range(tiles - 2, -1, -1):
        attend(i)

    @pl.loop(1, n)
    def _(k):
        back(k).wait_recv()

    @pl.loop(0, heads)
    def _(h):
        gain = gain_ref[:, lanes(h)]
        for i in range(tiles):
            lo, hi = i * B, (i + 1) * B
            far = jnp.dot(
                phi[0, lo:hi, lanes(h)], carried[lanes(h), :], preferred_element_type=F32
            )
            whole = mix[lo:hi, lanes(h)] + far * masks[3, lo:hi, :]
            power = jnp.mean(whole * whole, axis=1, keepdims=True)
            out_ref[lo:hi, lanes(h)] = (whole * lax.rsqrt(power + 1e-6) * gain).astype(BF16)

    for w in range(3):
        halo(w).wait_send()

    @pl.loop(1, n)
    def _(k):
        give(k).wait_send()
        back(k).wait_send()


def per_device(n, query_rows, key_rows, value_rows, lengths, conv_weight, out_gain):
    T, width = query_rows.shape
    anywhere = pl.BlockSpec(memory_space=pl.ANY)
    vmem = pl.BlockSpec(memory_space=pltpu.VMEM)
    return pl.pallas_call(
        functools.partial(kernel, n),
        out_shape=jax.ShapeDtypeStruct((T, width), BF16),
        in_specs=[anywhere] * 3 + [vmem] * 3,
        out_specs=vmem,
        scratch_shapes=[
            pltpu.VMEM((3, T + PAD, width), BF16),
            pltpu.VMEM((3, T, width), BF16),
            pltpu.VMEM((T, width), F32),
            pltpu.VMEM((4, T, HEAD), F32),
            pltpu.VMEM((T, T), BF16),
            pltpu.VMEM((width, HEAD), BF16),
            pltpu.VMEM((width, HEAD), BF16),
            pltpu.VMEM((width, HEAD), BF16),
            pltpu.VMEM((width, HEAD), BF16),
            pltpu.SemaphoreType.DMA((3,)),
            pltpu.SemaphoreType.DMA((3,)),
            pltpu.SemaphoreType.DMA((3,)),
            pltpu.SemaphoreType.DMA((2, n)),
            pltpu.SemaphoreType.DMA((2, n)),
        ],
        compiler_params=pltpu.CompilerParams(
            collective_id=0, has_side_effects=True, vmem_limit_bytes=52 * 1024 * 1024
        ),
    )(
        query_rows, key_rows, value_rows, lengths.reshape(1, -1), conv_weight,
        out_gain.reshape(1, -1),
    )


def solution(mesh):
    return jax.shard_map(
        functools.partial(per_device, mesh.shape["ctx"]),
        mesh=mesh,
        in_specs=(
            P(("dp", "ctx"), None),
            P(("dp", "ctx"), None),
            P(("dp", "ctx"), None),
            P("dp"),
            P(),
            P(),
        ),
        out_specs=P(("dp", "ctx"), None),
        check_vma=False,
    )
```

time: 152 us -> 45 us (0.30)
  the two profiles are of different devices: /device:TPU:24 before, /device:TPU:0 now
where the time goes in v1:
time: 45 us; the launch traced here: 44.8 us
  Pallas kernels  39.6 us (88%)
  local copies, waits for them, and re-layouts  5.22 us (12%)
    pallas_call x1, Pallas kernels, per_device(): pl.pallas_call(functools.partial(kernel, n), out_shape=jax.ShapeDtypeStru...  39.6 us
    unnamed x7, local copies, waits for them, and re-layouts  5.22 us

profile of v1, /device:TPU:0, one launch (start us, length us, event | category | flops | bytes accessed | tf_op | source)
XLA Modules:
  0.0 44.8 jit_solution(2289330221506672125)
XLA Ops:
  0.0 0.0 copy-start
  0.0 0.8 %copy-done = f32[3,4,1024]{2,1,0:T(4,128)S(1)} copy-done((f32[3,4,1024]{2,1,0:T(4,128)S(1)}, f32[3,4,1024]{2,1,0:T(4,128)}, u32[]{:S(2)}) %copy-start) | copy-done | bytes 49176
  0.8 0.0 copy-start.1
  0.8 0.7 %copy-done.1 = f32[1024]{0:T(1024)S(1)} copy-done((f32[1024]{0:T(1024)S(1)}, f32[1024]{0:T(1024)}, u32[]{:S(2)}) %copy-start.1) | copy-done | bytes 4120
  1.5 0.0 copy-start.2
  1.5 0.7 %copy-done.2 = s32[32]{0:T(128)S(1)} copy-done((s32[32]{0:T(128)S(1)}, s32[32]{0:T(128)}, u32[]{:S(2)}) %copy-start.2) | copy-done | bytes 152
  2.1 39.6 %shard_map.64 = bf16[1024,1024]{1,0:T(8,128)(2,1)} custom-call(bf16[1024,1024]{1,0:T(8,128)(2,1)} %q_hbm.1, bf16[1024,1024]{1,0:T(8,128)(2,1)} %k_hbm.1, bf16[1024,1024]{1,0:T(8,128)(2,1)} %v_hbm.1, s32[1,32]{1,0:T(1,128)S(1)} %bitcast.3, f32[3,4,1024]{2,1,0:T(4,128)S(1)} %copy-done, f32[1,1024]{1,0:T(1,128)S(1)} %bitcast.2), custom_call_target="tpu_custom_call" | custom-call | tf_op jit(solution)/shard_map/pallas_call | solution.py:252
  41.7 3.1 %copy.8 = bf16[1024,1024]{1,0:T(8,128)(2,1)} copy(bf16[1024,1024]{1,0:T(8,128)(2,1)} %shard_map.64) | data formatting | bytes 4194304
Async XLA Ops:
  0.0 0.8 %copy-start = (f32[3,4,1024]{2,1,0:T(4,128)S(1)}, f32[3,4,1024]{2,1,0:T(4,128)}, u32[]{:S(2)}) copy-start(f32[3,4,1024]{2,1,0:T(4,128)} %cw_ref.1) | copy-start | bytes 147460
  0.8 0.7 %copy-start.1 = (f32[1024]{0:T(1024)S(1)}, f32[1024]{0:T(1024)}, u32[]{:S(2)}) copy-start(f32[1024]{0:T(1024)} %param.11) | copy-start | bytes 12292
  1.5 0.7 %copy-start.2 = (s32[32]{0:T(128)S(1)}, s32[32]{0:T(128)}, u32[]{:S(2)}) copy-start(s32[32]{0:T(128)} %param.9) | copy-start | bytes 388

commit v2 on v1

v2 whole, which is shorter than its diff:
```python
import functools

import jax
import jax.numpy as jnp
from jax import lax
from jax.experimental import pallas as pl
from jax.experimental.pallas import tpu as pltpu
from jax.sharding import PartitionSpec as P

HEAD = 128
PAD = 16
B = 256
MESH = pl.DeviceIdType.MESH
F32 = jnp.float32
BF16 = jnp.bfloat16


def lanes(head):
    return pl.ds(pl.multiple_of(head * HEAD, HEAD), HEAD)


def iota(shape, dim):
    return lax.broadcasted_iota(jnp.int32, shape, dim).astype(F32)


def kernel(
    n, q_hbm, k_hbm, v_hbm, len_ref, cw_ref, mix_hbm, far_hbm, state_ref,
    rows_in, phi, mix, masks, allow, keeps, within, tail, gathered, scanned, carried,
    load_sem, halo_send, halo_recv, send_sem, recv_sem, mix_sem, far_sem,
):
    me = lax.axis_index("ctx")
    T, width = q_hbm.shape
    heads = width // HEAD
    R = width // n
    per = n // heads
    ndoc = len_ref.shape[1]
    tiles = T // B
    inputs = (q_hbm, k_hbm, v_hbm)

    def load(w):
        return pltpu.make_async_copy(inputs[w], rows_in.at[w, pl.ds(PAD, T)], load_sem.at[w])

    for w in (1, 2, 0):
        load(w).start()

    barrier = pltpu.get_barrier_semaphore()

    @pl.loop(1, n)
    def _(k):
        pl.semaphore_signal(
            barrier, inc=1, device_id={"ctx": lax.rem(me + k, n)}, device_id_type=MESH
        )

    sub = lax.broadcasted_iota(jnp.int32, (ndoc, ndoc), 0)
    lan = lax.broadcasted_iota(jnp.int32, (ndoc, ndoc), 1)
    lens = len_ref[...].astype(F32)
    col = jnp.sum(jnp.where(lan < sub, lens, 0.0), axis=1, keepdims=True)
    starts = jnp.sum(jnp.where(lan == sub, col, 0.0), axis=0, keepdims=True)
    offset = (me * T).astype(F32)

    first = iota((n, ndoc), 0) * T
    inside = (starts >= first) & (starts < first + T)
    hit = jnp.max(jnp.where(inside, 1.0, 0.0), axis=1, keepdims=True)
    keeps[...] = jnp.broadcast_to(1.0 - hit, (n, HEAD))

    MC = 128
    for c in range(T // MC):
        r0 = c * MC
        local = iota((MC, 1), 0) + r0
        pos = local + offset
        mine = jnp.max(jnp.where(starts <= pos, starts, -1.0), axis=1, keepdims=True)
        depth = jnp.broadcast_to(pos - mine, (MC, HEAD))
        rows = pl.ds(r0, MC)
        for j in range(1, 4):
            masks[j - 1, rows, :] = (depth >= j).astype(F32)
        masks[3, rows, :] = (depth > local).astype(F32)
        opening = (r0 // B) * B
        masks[4, rows, :] = (depth > local - opening).astype(F32)
        for piece in range(B // HEAD):
            gap = local - (iota((MC, HEAD), 1) + (opening + piece * HEAD))
            ok = (gap >= 0.0) & (gap <= depth)
            allow[rows, piece * HEAD : (piece + 1) * HEAD] = jnp.where(ok, 1.0, 0.0).astype(BF16)

    def last_start(c):
        end = offset + ((c + 1) * B - 1)
        return jnp.max(jnp.where(starts <= end, starts, -1.0), axis=1, keepdims=True)

    lasts = [last_start(c) - offset for c in range(tiles)]
    goes_on = [(lasts[c] < c * B).astype(F32) for c in range(tiles)]

    nxt = lax.rem(me + 1, n)

    def halo(w):
        return pltpu.make_async_remote_copy(
            src_ref=inputs[w].at[pl.ds(T - PAD, PAD)],
            dst_ref=rows_in.at[w, pl.ds(0, PAD)],
            send_sem=halo_send.at[w],
            recv_sem=halo_recv.at[w],
            device_id={"ctx": nxt},
            device_id_type=MESH,
        )

    pl.semaphore_wait(barrier, n - 1)
    for w in (1, 2, 0):
        halo(w).start()

    C = 128
    chunks = T // C

    def conv(w, h, c):
        rows = pl.ds(c * C, C)
        ext = rows_in[w, pl.ds(c * C, C + PAD), lanes(h)].astype(F32)
        scale = 1.0 if w == 2 else 0.5
        acc = ext[PAD:] * (cw_ref[w, 0:1, lanes(h)] * scale)
        for j in range(1, 4):
            tap = cw_ref[w, j : j + 1, lanes(h)] * scale
            acc += (ext[PAD - j : PAD - j + C] * masks[j - 1, rows, :]) * tap
        if w < 2:
            acc = acc + acc * jnp.tanh(acc)
        phi[w, rows, lanes(h)] = acc.astype(BF16)

    def slice_rows(d):
        return pl.ds(pl.multiple_of(d * R, R), R)

    def give(k):
        to = lax.rem(me + k, n)
        return pltpu.make_async_remote_copy(
            src_ref=tail.at[slice_rows(to)],
            dst_ref=gathered.at[slice_rows(me)],
            send_sem=send_sem.at[0, k],
            recv_sem=recv_sem.at[0, k],
            device_id={"ctx": to},
            device_id_type=MESH,
        )

    def back(k):
        to = lax.rem(me + k, n)
        return pltpu.make_async_remote_copy(
            src_ref=scanned.at[slice_rows(to)],
            dst_ref=carried.at[slice_rows(me)],
            send_sem=send_sem.at[1, k],
            recv_sem=recv_sem.at[1, k],
            device_id={"ctx": to},
            device_id_type=MESH,
        )

    def order(i):
        return lax.rem(me // per + 1 + i, heads)

    EARLY = 2
    load(1).wait()
    load(2).wait()

    @pl.loop(0, EARLY)
    def _(i):
        for c in range(chunks - 1, 0, -1):
            conv(1, order(i), c)
            conv(2, order(i), c)

    halo(1).wait_recv()
    halo(2).wait_recv()

    @pl.loop(0, heads)
    def _(i):
        h = order(i)

        @pl.when(i >= EARLY)
        def _():
            for c in range(chunks - 1, 0, -1):
                conv(1, h, c)
                conv(2, h, c)

        conv(1, h, 0)
        conv(2, h, 0)
        state = None
        for c in range(tiles):
            rows = slice(c * B, (c + 1) * B)
            live = (iota((B, HEAD), 0) + c * B) >= lasts[c]
            key = jnp.where(live, phi[1, rows, lanes(h)].astype(F32), 0.0).astype(BF16)
            own = lax.dot_general(
                key, phi[2, rows, lanes(h)], (((0,), (0,)), ((), ())), preferred_element_type=F32
            )
            state = own if state is None else state * goes_on[c] + own
            if c < tiles - 1:
                within[c, lanes(h), :] = state.astype(BF16)
        tail[lanes(h), :] = state.astype(BF16)

        @pl.loop(0, per)
        def _(j):
            k = lax.rem(h * per + j - me + n, n)

            @pl.when(k != 0)
            def _():
                give(k).start()

    gathered[slice_rows(me), :] = tail[slice_rows(me), :]

    load(0).wait()
    halo(0).wait_recv()

    def conv_q(h):
        for c in range(chunks):
            conv(0, h, c)

    pl.loop(0, heads // 2)(conv_q)

    @pl.loop(1, n)
    def _(k):
        give(k).wait_recv()

    def step(b, state):
        scanned[slice_rows(b), :] = state.astype(BF16)
        return state * keeps[pl.ds(b, 1), :] + gathered[slice_rows(b), :].astype(F32)

    lax.fori_loop(0, n, step, jnp.zeros((R, HEAD), F32), unroll=4)

    @pl.loop(1, n)
    def _(k):
        back(k).start()

    carried[slice_rows(me), :] = scanned[slice_rows(me), :]

    pl.loop(heads // 2, heads)(conv_q)

    def mix_out(i):
        rows = pl.ds(i * B, B)
        return pltpu.make_async_copy(mix.at[rows], mix_hbm.at[rows], mix_sem.at[i])

    def far_out(i):
        rows = pl.ds(i * B, B)
        return pltpu.make_async_copy(rows_in.at[0, rows], far_hbm.at[rows], far_sem.at[i])

    halo(0).wait_send()
    for i in range(tiles):
        lo, hi = i * B, (i + 1) * B

        @pl.loop(0, heads, unroll=4)
        def _(h):
            query = phi[0, lo:hi, lanes(h)]
            score = lax.dot_general(
                query, phi[1, lo:hi, lanes(h)],
                (((1,), (1,)), ((), ())), preferred_element_type=F32,
            )
            weights = score.astype(BF16) * allow[lo:hi, :]
            got = jnp.dot(weights, phi[2, lo:hi, lanes(h)], preferred_element_type=F32)
            wide = query.astype(F32)
            if i:
                seen = (wide * masks[4, lo:hi, :]).astype(BF16)
                got += jnp.dot(seen, within[i - 1, lanes(h), :], preferred_element_type=F32)
            mix[lo:hi, lanes(h)] = got
            rows_in[0, lo:hi, lanes(h)] = (wide * masks[3, lo:hi, :]).astype(BF16)

        mix_out(i).start()
        far_out(i).start()

    @pl.loop(1, n)
    def _(k):
        back(k).wait_recv()

    state_ref[...] = carried[...]

    for w in (1, 2):
        halo(w).wait_send()

    @pl.loop(1, n)
    def _(k):
        give(k).wait_send()
        back(k).wait_send()

    for i in range(tiles):
        mix_out(i).wait()
        far_out(i).wait()


def finish(mix_ref, far_ref, state_ref, gain_ref, out_ref):
    for h in range(mix_ref.shape[1] // HEAD):
        cols = slice(h * HEAD, (h + 1) * HEAD)
        whole = mix_ref[:, cols] + jnp.dot(
            far_ref[:, cols], state_ref[cols, :], preferred_element_type=F32
        )
        power = jnp.mean(whole * whole, axis=1, keepdims=True)
        out_ref[:, cols] = (whole * lax.rsqrt(power + 1e-6) * gain_ref[:, cols]).astype(BF16)


def per_device(n, query_rows, key_rows, value_rows, lengths, conv_weight, out_gain):
    T, width = query_rows.shape
    anywhere = pl.BlockSpec(memory_space=pl.ANY)
    vmem = pl.BlockSpec(memory_space=pltpu.VMEM)
    tiles = T // B
    mix, far, state = pl.pallas_call(
        functools.partial(kernel, n),
        out_shape=(
            jax.ShapeDtypeStruct((T, width), F32),
            jax.ShapeDtypeStruct((T, width), BF16),
            jax.ShapeDtypeStruct((width, HEAD), BF16),
        ),
        in_specs=[anywhere] * 3 + [vmem] * 2,
        out_specs=(anywhere, anywhere, vmem),
        scratch_shapes=[
            pltpu.VMEM((3, T + PAD, width), BF16),
            pltpu.VMEM((3, T, width), BF16),
            pltpu.VMEM((T, width), F32),
            pltpu.VMEM((5, T, HEAD), F32),
            pltpu.VMEM((T, B), BF16),
            pltpu.VMEM((n, HEAD), F32),
            pltpu.VMEM((tiles - 1, width, HEAD), BF16),
            pltpu.VMEM((width, HEAD), BF16),
            pltpu.VMEM((width, HEAD), BF16),
            pltpu.VMEM((width, HEAD), BF16),
            pltpu.VMEM((width, HEAD), BF16),
            pltpu.SemaphoreType.DMA((3,)),
            pltpu.SemaphoreType.DMA((3,)),
            pltpu.SemaphoreType.DMA((3,)),
            pltpu.SemaphoreType.DMA((2, n)),
            pltpu.SemaphoreType.DMA((2, n)),
            pltpu.SemaphoreType.DMA((tiles,)),
            pltpu.SemaphoreType.DMA((tiles,)),
        ],
        compiler_params=pltpu.CompilerParams(
            collective_id=0, has_side_effects=True, vmem_limit_bytes=62 * 1024 * 1024
        ),
    )(query_rows, key_rows, value_rows, lengths.reshape(1, -1), conv_weight)
    tile = pl.BlockSpec((B, width), lambda i: (i, 0))
    return pl.pallas_call(
        finish,
        grid=(tiles,),
        out_shape=jax.ShapeDtypeStruct((T, width), BF16),
        in_specs=[
            tile,
            tile,
            pl.BlockSpec((width, HEAD), lambda i: (0, 0)),
            pl.BlockSpec((1, width), lambda i: (0, 0)),
        ],
        out_specs=tile,
        compiler_params=pltpu.CompilerParams(vmem_limit_bytes=62 * 1024 * 1024),
    )(mix, far, state, out_gain.reshape(1, -1))


def solution(mesh):
    return jax.shard_map(
        functools.partial(per_device, mesh.shape["ctx"]),
        mesh=mesh,
        in_specs=(
            P(("dp", "ctx"), None),
            P(("dp", "ctx"), None),
            P(("dp", "ctx"), None),
            P("dp"),
            P(),
            P(),
        ),
        out_specs=P(("dp", "ctx"), None),
        check_vma=False,
    )
```

time: 45 us -> 35.5 us (0.79)
  local copies, waits for them, and re-layouts: 5.22 us -> 0 us
  Pallas kernels: 39.6 us -> 35.3 us
    unnamed x7 -> x0, local copies, waits for them, and re-layouts: 5.22 us -> none
    pallas_call x1 -> x2, Pallas kernels: 39.6 us -> 35.3 us  [the longest x1 29.7 us: per_device(): pl.pallas_call(functools.partial(kernel, n), out_shape=(jax.ShapeDtypeStr...]
where the time goes in v2:
time: 35.5 us; the launch traced here: 35.3 us
  Pallas kernels  35.3 us (99%)
    pallas_call x1, Pallas kernels, per_device(): pl.pallas_call(functools.partial(kernel, n), out_shape=(jax.ShapeDtypeStr...  29.7 us
    pallas_call x1, Pallas kernels, per_device(): pl.pallas_call(finish, grid=(tiles,), out_shape=jax.ShapeDtypeStruct((T,...  5.58 us

profile of v2, /device:TPU:0, one launch (start us, length us, event | category | flops | bytes accessed | tf_op | source)
XLA Modules:
  0.0 35.3 jit_solution(1538870850400876371)
XLA Ops:
  0.0 29.7 %shard_map.64 = (f32[1024,1024]{1,0:T(8,128)}, bf16[1024,1024]{1,0:T(8,128)(2,1)}, bf16[1024,128]{1,0:T(8,128)(2,1)}) custom-call(bf16[1024,1024]{1,0:T(8,128)(2,1)} %q_hbm.1, bf16[1024,1024]{1,0:T(8,128)(2,1)} %k_hbm.1, bf16[1024,1024]{1,0:T(8,128)(2,1)} %v_hbm.1, s32[1,32]{1,0:T(1,128)} %bitcast.3, f32[3,4,1024]{2,1,0:T(4,128)} %cw_ref.1), custom_call_target="tpu_custom_call" | custom-call | tf_op jit(solution)/shard_map/pallas_call | solution.py:290
  29.8 5.6 %shard_map.65 = bf16[1024,1024]{1,0:T(8,128)(2,1)} custom-call(f32[1024,1024]{1,0:T(8,128)} %get-tuple-element.8.mix_ref, bf16[1024,1024]{1,0:T(8,128)(2,1)} %get-tuple-element.9.far_ref, bf16[1024,128]{1,0:T(8,128)(2,1)} %get-tuple-element.10.state_ref, f32[1,1024]{1,0:T(1,128)} %bitcast.2), custom_call_target="tpu_custom_call" | custom-call | tf_op jit(solution)/shard_map/pallas_call | solution.py:324

commit v3 on v2

--- a/solution.py
+++ b/solution.py
@@ -8,7 +8,8 @@
 from jax.sharding import PartitionSpec as P
 
 HEAD = 128
-PAD = 16
+PAD = 128
+EDGE = 16
 B = 256
 MESH = pl.DeviceIdType.MESH
 F32 = jnp.float32
@@ -25,7 +26,7 @@
 
 def kernel(
     n, q_hbm, k_hbm, v_hbm, len_ref, cw_ref, mix_hbm, far_hbm, state_ref,
-    rows_in, phi, mix, masks, allow, keeps, within, tail, gathered, scanned, carried,
+    rows_in, phi, mix, masks, shifts, allow, keeps, within, tail, gathered, scanned, carried,
     load_sem, halo_send, halo_recv, send_sem, recv_sem, mix_sem, far_sem,
 ):
     me = lax.axis_index("ctx")
@@ -71,11 +72,14 @@
         mine = jnp.max(jnp.where(starts <= pos, starts, -1.0), axis=1, keepdims=True)
         depth = jnp.broadcast_to(pos - mine, (MC, HEAD))
         rows = pl.ds(r0, MC)
+        wide = jnp.concatenate([depth, depth], axis=1)
+        away = iota((MC, 2 * HEAD), 0) + PAD - iota((MC, 2 * HEAD), 1)
         for j in range(1, 4):
-            masks[j - 1, rows, :] = (depth >= j).astype(F32)
-        masks[3, rows, :] = (depth > local).astype(F32)
+            here = (away == j) & (wide >= j)
+            shifts[c, (j - 1) * MC : j * MC, :] = jnp.where(here, 1.0, 0.0).astype(BF16)
+        masks[0, rows, :] = (depth > local).astype(F32)
         opening = (r0 // B) * B
-        masks[4, rows, :] = (depth > local - opening).astype(F32)
+        masks[1, rows, :] = (depth > local - opening).astype(F32)
         for piece in range(B // HEAD):
             gap = local - (iota((MC, HEAD), 1) + (opening + piece * HEAD))
             ok = (gap >= 0.0) & (gap <= depth)
@@ -92,14 +96,17 @@
 
     def halo(w):
         return pltpu.make_async_remote_copy(
-            src_ref=inputs[w].at[pl.ds(T - PAD, PAD)],
-            dst_ref=rows_in.at[w, pl.ds(0, PAD)],
+            src_ref=inputs[w].at[pl.ds(T - EDGE, EDGE)],
+            dst_ref=rows_in.at[w, pl.ds(PAD - EDGE, EDGE)],
             send_sem=halo_send.at[w],
             recv_sem=halo_recv.at[w],
             device_id={"ctx": nxt},
             device_id_type=MESH,
         )
 
+    for w in range(3):
+        rows_in[w, 0 : PAD - EDGE, :] = jnp.zeros((PAD - EDGE, width), BF16)
+
     pl.semaphore_wait(barrier, n - 1)
     for w in (1, 2, 0):
         halo(w).start()
@@ -107,17 +114,20 @@
     C = 128
     chunks = T // C
 
-    def conv(w, h, c):
+    def conv(w, pair, c):
         rows = pl.ds(c * C, C)
-        ext = rows_in[w, pl.ds(c * C, C + PAD), lanes(h)].astype(F32)
+        cols = pl.ds(pl.multiple_of(pair * 2 * HEAD, 2 * HEAD), 2 * HEAD)
+        moved = jnp.dot(
+            shifts[c], rows_in[w, pl.ds(c * C, C + PAD), cols], preferred_element_type=F32
+        )
         scale = 1.0 if w == 2 else 0.5
-        acc = ext[PAD:] * (cw_ref[w, 0:1, lanes(h)] * scale)
+        now = rows_in[w, pl.ds(c * C + PAD, C), cols].astype(F32)
+        acc = now * (cw_ref[w, 0:1, cols] * scale)
         for j in range(1, 4):
-            tap = cw_ref[w, j : j + 1, lanes(h)] * scale
-            acc += (ext[PAD - j : PAD - j + C] * masks[j - 1, rows, :]) * tap
+            acc += moved[(j - 1) * C : j * C] * (cw_ref[w, j : j + 1, cols] * scale)
         if w < 2:
             acc = acc + acc * jnp.tanh(acc)
-        phi[w, rows, lanes(h)] = acc.astype(BF16)
+        phi[w, rows, cols] = acc.astype(BF16)
 
     def slice_rows(d):
         return pl.ds(pl.multiple_of(d * R, R), R)
@@ -145,9 +155,9 @@
         )
 
     def order(i):
-        return lax.rem(me // per + 1 + i, heads)
-
-    EARLY = 2
+        return lax.rem(me // (2 * per) + 1 + i, heads // 2)
+
+    EARLY = 1
     load(1).wait()
     load(2).wait()
 
@@ -160,34 +170,37 @@
     halo(1).wait_recv()
     halo(2).wait_recv()
 
-    @pl.loop(0, heads)
+    @pl.loop(0, heads // 2)
     def _(i):
-        h = order(i)
+        pair = order(i)
 
         @pl.when(i >= EARLY)
         def _():
             for c in range(chunks - 1, 0, -1):
-                conv(1, h, c)
-                conv(2, h, c)
-
-        conv(1, h, 0)
-        conv(2, h, 0)
-        state = None
-        for c in range(tiles):
-            rows = slice(c * B, (c + 1) * B)
-            live = (iota((B, HEAD), 0) + c * B) >= lasts[c]
-            key = jnp.where(live, phi[1, rows, lanes(h)].astype(F32), 0.0).astype(BF16)
-            own = lax.dot_general(
-                key, phi[2, rows, lanes(h)], (((0,), (0,)), ((), ())), preferred_element_type=F32
-            )
-            state = own if state is None else state * goes_on[c] + own
-            if c < tiles - 1:
-                within[c, lanes(h), :] = state.astype(BF16)
-        tail[lanes(h), :] = state.astype(BF16)
-
-        @pl.loop(0, per)
+                conv(1, pair, c)
+                conv(2, pair, c)
+
+        conv(1, pair, 0)
+        conv(2, pair, 0)
+        for one in range(2):
+            h = pair * 2 + one
+            state = None
+            for c in range(tiles):
+                rows = slice(c * B, (c + 1) * B)
+                live = (iota((B, HEAD), 0) + c * B) >= lasts[c]
+                key = jnp.where(live, phi[1, rows, lanes(h)].astype(F32), 0.0).astype(BF16)
+                own = lax.dot_general(
+                    key, phi[2, rows, lanes(h)], (((0,), (0,)), ((), ())),
+                    preferred_element_type=F32,
+                )
+                state = own if state is None else state * goes_on[c] + own
+                if c < tiles - 1:
+                    within[c, lanes(h), :] = state.astype(BF16)
+            tail[lanes(h), :] = state.astype(BF16)
+
+        @pl.loop(0, 2 * per)
         def _(j):
-            k = lax.rem(h * per + j - me + n, n)
+            k = lax.rem(pair * 2 * per + j - me + n, n)
 
             @pl.when(k != 0)
             def _():
@@ -202,7 +215,7 @@
         for c in range(chunks):
             conv(0, h, c)
 
-    pl.loop(0, heads // 2)(conv_q)
+    pl.loop(0, EARLY)(conv_q)
 
     @pl.loop(1, n)
     def _(k):
@@ -220,7 +233,7 @@
 
     carried[slice_rows(me), :] = scanned[slice_rows(me), :]
 
-    pl.loop(heads // 2, heads)(conv_q)
+    pl.loop(EARLY, heads // 2)(conv_q)
 
     def mix_out(i):
         rows = pl.ds(i * B, B)
@@ -245,10 +258,10 @@
             got = jnp.dot(weights, phi[2, lo:hi, lanes(h)], preferred_element_type=F32)
             wide = query.astype(F32)
             if i:
-                seen = (wide * masks[4, lo:hi, :]).astype(BF16)
+                seen = (wide * masks[1, lo:hi, :]).astype(BF16)
                 got += jnp.dot(seen, within[i - 1, lanes(h), :], preferred_element_type=F32)
             mix[lo:hi, lanes(h)] = got
-            rows_in[0, lo:hi, lanes(h)] = (wide * masks[3, lo:hi, :]).astype(BF16)
+            rows_in[0, lo:hi, lanes(h)] = (wide * masks[0, lo:hi, :]).astype(BF16)
 
         mix_out(i).start()
         far_out(i).start()
@@ -273,12 +286,14 @@
 
 
 def finish(mix_ref, far_ref, state_ref, gain_ref, out_ref):
+    average = jnp.full((HEAD, HEAD), 1.0 / HEAD, BF16)
     for h in range(mix_ref.shape[1] // HEAD):
         cols = slice(h * HEAD, (h + 1) * HEAD)
         whole = mix_ref[:, cols] + jnp.dot(
             far_ref[:, cols], state_ref[cols, :], preferred_element_type=F32
         )
-        power = jnp.mean(whole * whole, axis=1, keepdims=True)
+        square = (whole * whole).astype(BF16)
+        power = jnp.dot(square, average, preferred_element_type=F32)
         out_ref[:, cols] = (whole * lax.rsqrt(power + 1e-6) * gain_ref[:, cols]).astype(BF16)
 
 
@@ -300,7 +315,8 @@
             pltpu.VMEM((3, T + PAD, width), BF16),
             pltpu.VMEM((3, T, width), BF16),
             pltpu.VMEM((T, width), F32),
-            pltpu.VMEM((5, T, HEAD), F32),
+            pltpu.VMEM((2, T, HEAD), F32),
+            pltpu.VMEM((T // 128, 384, 2 * HEAD), BF16),
             pltpu.VMEM((T, B), BF16),
             pltpu.VMEM((n, HEAD), F32),
             pltpu.VMEM((tiles - 1, width, HEAD), BF16),

time: 35.5 us -> 34.8 us (0.980)
  Pallas kernels: 35.3 us -> 34.6 us
    pallas_call x1, Pallas kernels: 29.7 us -> 28.9 us  [per_device(): pl.pallas_call(functools.partial(kernel, n), out_shape=(jax.ShapeDtypeStr...]
where the time goes in v3:
time: 34.8 us; the launch traced here: 34.6 us
  Pallas kernels  34.6 us (99%)
    pallas_call x1, Pallas kernels, per_device(): pl.pallas_call(functools.partial(kernel, n), out_shape=(jax.ShapeDtypeStr...  28.9 us
    pallas_call x1, Pallas kernels, per_device(): pl.pallas_call(finish, grid=(tiles,), out_shape=jax.ShapeDtypeStruct((T,...  5.64 us

profile of v3, /device:TPU:0, one launch (start us, length us, event | category | flops | bytes accessed | tf_op | source)
XLA Modules:
  0.0 34.6 jit_solution(1011234725074780579)
XLA Ops:
  0.0 28.9 %shard_map.64 = (f32[1024,1024]{1,0:T(8,128)}, bf16[1024,1024]{1,0:T(8,128)(2,1)}, bf16[1024,128]{1,0:T(8,128)(2,1)}) custom-call(bf16[1024,1024]{1,0:T(8,128)(2,1)} %q_hbm.1, bf16[1024,1024]{1,0:T(8,128)(2,1)} %k_hbm.1, bf16[1024,1024]{1,0:T(8,128)(2,1)} %v_hbm.1, s32[1,32]{1,0:T(1,128)} %bitcast.3, f32[3,4,1024]{2,1,0:T(4,128)} %cw_ref.1), custom_call_target="tpu_custom_call" | custom-call | tf_op jit(solution)/shard_map/pallas_call | solution.py:305
  28.9 5.6 %shard_map.65 = bf16[1024,1024]{1,0:T(8,128)(2,1)} custom-call(f32[1024,1024]{1,0:T(8,128)} %get-tuple-element.8.mix_ref, bf16[1024,1024]{1,0:T(8,128)(2,1)} %get-tuple-element.9.far_ref, bf16[1024,128]{1,0:T(8,128)(2,1)} %get-tuple-element.10.state_ref, f32[1,1024]{1,0:T(1,128)} %bitcast.2), custom_call_target="tpu_custom_call" | custom-call | tf_op jit(solution)/shard_map/pallas_call | solution.py:340

commit v4 on v3

--- a/solution.py
+++ b/solution.py
@@ -260,7 +260,7 @@
             if i:
                 seen = (wide * masks[1, lo:hi, :]).astype(BF16)
                 got += jnp.dot(seen, within[i - 1, lanes(h), :], preferred_element_type=F32)
-            mix[lo:hi, lanes(h)] = got
+            mix[lo:hi, lanes(h)] = got.astype(BF16)
             rows_in[0, lo:hi, lanes(h)] = (wide * masks[0, lo:hi, :]).astype(BF16)
 
         mix_out(i).start()
@@ -289,7 +289,7 @@
     average = jnp.full((HEAD, HEAD), 1.0 / HEAD, BF16)
     for h in range(mix_ref.shape[1] // HEAD):
         cols = slice(h * HEAD, (h + 1) * HEAD)
-        whole = mix_ref[:, cols] + jnp.dot(
+        whole = mix_ref[:, cols].astype(F32) + jnp.dot(
             far_ref[:, cols], state_ref[cols, :], preferred_element_type=F32
         )
         square = (whole * whole).astype(BF16)
@@ -305,7 +305,7 @@
     mix, far, state = pl.pallas_call(
         functools.partial(kernel, n),
         out_shape=(
-            jax.ShapeDtypeStruct((T, width), F32),
+            jax.ShapeDtypeStruct((T, width), BF16),
             jax.ShapeDtypeStruct((T, width), BF16),
             jax.ShapeDtypeStruct((width, HEAD), BF16),
         ),
@@ -314,7 +314,7 @@
         scratch_shapes=[
             pltpu.VMEM((3, T + PAD, width), BF16),
             pltpu.VMEM((3, T, width), BF16),
-            pltpu.VMEM((T, width), F32),
+            pltpu.VMEM((T, width), BF16),
             pltpu.VMEM((2, T, HEAD), F32),
             pltpu.VMEM((T // 128, 384, 2 * HEAD), BF16),
             pltpu.VMEM((T, B), BF16),

time: 34.8 us -> 34.2 us (0.983)
  Pallas kernels: 34.6 us -> 34 us
    pallas_call x1, Pallas kernels: 5.64 us -> 5.25 us  [per_device(): pl.pallas_call(finish, grid=(tiles,), out_shape=jax.ShapeDtypeStruct((T,...]
where the time goes in v4:
time: 34.2 us; the launch traced here: 34 us
  Pallas kernels  34 us (99%)
    pallas_call x1, Pallas kernels, per_device(): pl.pallas_call(functools.partial(kernel, n), out_shape=(jax.ShapeDtypeStr...  28.7 us
    pallas_call x1, Pallas kernels, per_device(): pl.pallas_call(finish, grid=(tiles,), out_shape=jax.ShapeDtypeStruct((T,...  5.25 us

profile of v4, /device:TPU:0, one launch (start us, length us, event | category | flops | bytes accessed | tf_op | source)
XLA Modules:
  0.0 34.0 jit_solution(10201684192846554380)
XLA Ops:
  0.0 28.7 %shard_map.64 = (bf16[1024,1024]{1,0:T(8,128)(2,1)}, bf16[1024,1024]{1,0:T(8,128)(2,1)}, bf16[1024,128]{1,0:T(8,128)(2,1)}) custom-call(bf16[1024,1024]{1,0:T(8,128)(2,1)} %q_hbm.1, bf16[1024,1024]{1,0:T(8,128)(2,1)} %k_hbm.1, bf16[1024,1024]{1,0:T(8,128)(2,1)} %v_hbm.1, s32[1,32]{1,0:T(1,128)} %bitcast.3, f32[3,4,1024]{2,1,0:T(4,128)} %cw_ref.1), custom_call_target="tpu_custom_call" | custom-call | tf_op jit(solution)/shard_map/pallas_call | solution.py:305
  28.7 5.3 %shard_map.65 = bf16[1024,1024]{1,0:T(8,128)(2,1)} custom-call(bf16[1024,1024]{1,0:T(8,128)(2,1)} %get-tuple-element.8.mix_ref, bf16[1024,1024]{1,0:T(8,128)(2,1)} %get-tuple-element.9.far_ref, bf16[1024,128]{1,0:T(8,128)(2,1)} %get-tuple-element.10.state_ref, f32[1,1024]{1,0:T(1,128)} %bitcast.2), custom_call_target="tpu_custom_call" | custom-call | tf_op jit(solution)/shard_map/pallas_call | solution.py:340
